TPU v7x, 32 devices: a whole 2x2x4 slice. The times are simulated.
32 devices in a mesh: ctx: 8 (over y, x, core), tp: 4 (over z).
Axes of the slice: x: 2, y: 2, z: 4, core: 2. Of those that a mesh axis runs over, the one named last changes fastest.
Arguments:
- query_feat: bfloat16 [8192, 8192], P('tp', 'ctx'), may hold values from -6 to 6
- key_feat: bfloat16 [8192, 8192], P('tp', 'ctx'), may hold values from -6 to 6
- value_feat: bfloat16 [8192, 8192], P('tp', 'ctx'), may hold values from -6 to 6
- short_filter: float32 [3, 3, 8192], P(None, None, 'tp'), may hold values from -3 to 3
- skip: float32 [8192], P('tp'), may hold values from -3 to 3
- decay_rate: float32 [64, 16], P('tp'), may hold values from 2.4414063e-05 to 0.04, as said below
- residue: float32 [64, 16], P('tp'), may hold values from -1 to 1
Outputs:
- regrouped: bfloat16 [64, 128, 8192], P('ctx', 'tp')
Inputs may be any that keep to these rules, and one draw needn't show every extreme that they name: `decay_rate`: positive decay rates of the modes.
All inputs are finite; a program needn't handle non-finite values.
Results may differ from a plain program's by a relative error of at most 0.001.
Values may be sent and summed in bfloat16 or wider, within the bound.
A program may use at most 128 MiB of HBM per device.

v0:
```python
import jax
import jax.numpy as jnp
from jax import lax
from jax.sharding import PartitionSpec as P


def shifted(x, axis, by):
    devices = lax.axis_size(axis)
    pairs = [(i, i + by) for i in range(devices) if 0 <= i + by < devices]
    return lax.ppermute(x, axis, pairs)


def near_head(inputs):
    rate, weight, products = inputs
    width = products.shape[1]
    middle = (width - 1.0) * 0.5
    spots = jnp.arange(width).astype(jnp.float32) - middle
    falling = weight[:, None] * jnp.exp(-rate[:, None] * spots[None, :])
    rising = jnp.exp(rate[:, None] * spots[None, :])
    full = lax.dot_general(
        falling, rising, (((0,), (0,)), ((), ())), precision=lax.Precision.HIGHEST
    )
    causal = lax.broadcasted_iota(jnp.int32, (width, width), 0) >= lax.broadcasted_iota(
        jnp.int32, (width, width), 1
    )
    toeplitz = jnp.where(causal, full, jnp.float32(0.0))
    return lax.dot_general(
        products, toeplitz, (((1,), (1,)), ((), ())), precision=lax.Precision.HIGHEST
    )


def per_device(query_feat, key_feat, value_feat, short_filter, skip, decay_rate, residue):
    stacked = jnp.stack([query_feat, key_feat, value_feat])
    before = shifted(stacked[:, :, -2:], "ctx", 1)
    extended = jnp.concatenate([before, stacked], axis=2).astype(jnp.float32)
    width = query_feat.shape[1]
    shorted = (
        short_filter[:, 0, :, None] * extended[:, :, 2:]
        + short_filter[:, 1, :, None] * extended[:, :, 1 : width + 1]
        + short_filter[:, 2, :, None] * extended[:, :, :width]
    )
    heads_here, modes = decay_rate.shape
    channels = query_feat.shape[0]
    head_width = channels // heads_here
    gate_heads = shorted[0].reshape(heads_here, head_width, width)
    products = (shorted[1] * shorted[2]).reshape(heads_here, head_width, width)
    near = lax.map(near_head, (decay_rate, residue, products))
    lag = jnp.arange(width).astype(jnp.float32)
    to_end = jnp.exp(-decay_rate[:, :, None] * (width - 1.0 - lag)[None, None, :])
    states = jnp.einsum("hns,hcs->hnc", to_end, products, precision=lax.Precision.HIGHEST)
    position = lax.axis_index("ctx").astype(jnp.float32)
    piece = lax.all_gather(states[None], "ctx", axis=0, tiled=True)
    count = piece.shape[0]
    source = jnp.arange(count).astype(jnp.float32)
    distance = position - 1.0 - source
    factor = jnp.exp(-decay_rate[None, :, :] * width * jnp.maximum(distance, 0.0)[:, None, None])
    factor = jnp.where(distance[:, None, None] >= 0.0, factor, jnp.float32(0.0))
    entering = jnp.einsum("khn,khnc->hnc", factor, piece, precision=lax.Precision.HIGHEST)
    from_start = residue[:, None, :] * jnp.exp(-decay_rate[:, None, :] * (lag[None, :, None] + 1.0))
    far = jnp.einsum("htn,hnc->hct", from_start, entering, precision=lax.Precision.HIGHEST)
    skip_heads = skip.reshape(heads_here, head_width)
    gated = (gate_heads * (near + far + skip_heads[:, :, None] * products)).astype(jnp.bfloat16)
    return lax.all_to_all(
        lax.all_to_all(gated, "tp", split_axis=1, concat_axis=0, tiled=True),
        "ctx",
        split_axis=0,
        concat_axis=2,
        tiled=True,
    )


def solution(mesh):
    return jax.shard_map(
        per_device,
        mesh=mesh,
        in_specs=(
            P("tp", "ctx"),
            P("tp", "ctx"),
            P("tp", "ctx"),
            P(None, None, "tp"),
            P("tp"),
            P("tp", None),
            P("tp", None),
        ),
        out_specs=P("ctx", "tp", None),
        check_vma=False,
    )
```

profile of v0, /device:TPU:11, one launch (start us, length us, event | category | flops | bytes accessed | tf_op | source)
XLA Modules:
  0.0 442.3 jit_solution(11640617810809966979)
XLA Ops:
  6.5 6.6 %copy.18 = bf16[2048,1024]{0,1:T(8,128)(2,1)} copy(bf16[2048,1024]{1,0:T(8,128)(2,1)} %param.9) | data formatting | bytes 8388608 | tf_op args[0]
  13.1 6.5 %copy.19 = bf16[2048,1024]{0,1:T(8,128)(2,1)} copy(bf16[2048,1024]{1,0:T(8,128)(2,1)} %param.10) | data formatting | bytes 8388608 | tf_op args[1]
  19.6 6.4 %copy.20 = bf16[2048,1024]{0,1:T(8,128)(2,1)} copy(bf16[2048,1024]{1,0:T(8,128)(2,1)} %param.11) | data formatting | bytes 8388608 | tf_op args[2]
  26.9 3.7 collective-permute-start
  31.5 14.9 %maximum_convert_fusion = f32[3,2048,1026]{1,2,0:T(8,128)} fusion(bf16[1,2048,1024]{1,2,0:T(8,128)(2,1)} %bitcast.55, bf16[1,2048,1024]{1,2,0:T(8,128)(2,1)} %bitcast.53, bf16[1,2048,1024]{1,2,0:T(8,128)(2,1)} %bitcast.51, bf16[3,2048,2]{1,2,0:T(2,128)(2,1)S(1)} %collective-permute-done), kind=kLoop, calls=%fused_computation.30 | loop fusion | flops 50429952 | bytes 37822464 | tf_op jit(solution)/shard_map/convert_element_type | solution.py:35
  46.4 33.9 %fusion.25 = f32[3,2048,1024]{1,2,0:T(8,128)} fusion(f32[3,2048,1026]{1,2,0:T(8,128)} %maximum_convert_fusion, f32[3,2048]{1,0:T(4,128)S(1)} %get-tuple-element.90, f32[3,2048]{1,0:T(4,128)S(1)} %get-tuple-element.91, f32[3,2048]{1,0:T(4,128)S(1)} %bitcast.62), kind=kLoop, calls=%fused_computation.26 | loop fusion | flops 31457280 | bytes 100737024 | tf_op jit(solution)/shard_map/add | solution.py:38
  80.3 14.9 %slice_multiply_fusion.3 = (f32[1,2048,1024]{1,2,0:T(8,128)}, f32[1,2048,1024]{1,2,0:T(8,128)}) fusion(f32[3,2048,1024]{1,2,0:T(8,128)} %fusion.25), kind=kLoop, calls=%fused_computation.31 | loop fusion | flops 2097152 | bytes 41943040 | tf_op jit(solution)/shard_map/mul | solution.py:46
  95.2 9.2 %copy.22 = f32[1,2048,1024]{2,1,0:T(8,128)} copy(f32[1,2048,1024]{1,2,0:T(8,128)} %get-tuple-element.83) | data formatting | bytes 16777216 | tf_op jit(solution)/shard_map/mul | solution.py:46
  104.5 10.1 %fusion.33 = f32[16,16,128]{2,1,0:T(8,128)} fusion(f32[16,128,1024]{2,1,0:T(8,128)} %bitcast.48, f32[1024]{0:T(1024)S(1)} %convert_subtract_fusion, f32[16,16]{1,0:T(8,128)S(1)} %get-tuple-element.88), kind=kOutput, calls=%fused_computation.39 | convolution fusion | flops 402915328 | bytes 8524800 | tf_op jit(solution)/shard_map/hns,hcs->hnc/dot_general | solution.py:50
  114.6 140.4 %while.12 = (s32[]{:T(128)}, f32[16,128,1024]{2,1,0:T(8,128)}, f32[16,128,1024]{2,1,0:T(8,128)}, f32[16,16]{1,0:T(8,128)S(1)}, f32[16,16]{1,0:T(8,128)S(1)}, /*index=5*/s32[]{:T(128)}) while((s32[]{:T(128)}, f32[16,128,1024]{2,1,0:T(8,128)}, f32[16,128,1024]{2,1,0:T(8,128)}, f32[16,16]{1,0:T(8,128)S(1)}, f32[16,16]{1,0:T(8,128)S(1)}, ...), condition=%wide.region_1.2_spmd, body=%wide.region_0.1_spmd.sunk | while | flops 1814087680 | bytes 9446989 | solution.py:47
  114.8 3.6 fusion.64
  118.4 5.1 %fusion.65 = f32[16,128,1024]{2,1,0:T(8,128)} fusion(f32[16,128,1024]{2,1,0:T(8,128)} %get-tuple-element.134, s32[]{:T(128)} %get-tuple-element.133, f32[1024,1024]{1,0:T(8,128)S(1)} %fusion.64, f32[16,128,1024]{2,1,0:T(8,128)} %get-tuple-element.141), kind=kOutput, calls=%fused_computation.5.clone.1 | convolution fusion | flops 1612709888 | bytes 5243904 | tf_op jit(solution)/shard_map/while/body/eval_jaxpr/dot_general | solution.py:27
  123.6 3.6 fusion.64
  127.2 5.1 %fusion.65 = f32[16,128,1024]{2,1,0:T(8,128)} fusion(f32[16,128,1024]{2,1,0:T(8,128)} %get-tuple-element.134, s32[]{:T(128)} %get-tuple-element.133, f32[1024,1024]{1,0:T(8,128)S(1)} %fusion.64, f32[16,128,1024]{2,1,0:T(8,128)} %get-tuple-element.141), kind=kOutput, calls=%fused_computation.5.clone.1 | convolution fusion | flops 1612709888 | bytes 5243904 | tf_op jit(solution)/shard_map/while/body/eval_jaxpr/dot_general | solution.py:27
  132.3 3.6 fusion.64
  135.9 5.1 %fusion.65 = f32[16,128,1024]{2,1,0:T(8,128)} fusion(f32[16,128,1024]{2,1,0:T(8,128)} %get-tuple-element.134, s32[]{:T(128)} %get-tuple-element.133, f32[1024,1024]{1,0:T(8,128)S(1)} %fusion.64, f32[16,128,1024]{2,1,0:T(8,128)} %get-tuple-element.141), kind=kOutput, calls=%fused_computation.5.clone.1 | convolution fusion | flops 1612709888 | bytes 5243904 | tf_op jit(solution)/shard_map/while/body/eval_jaxpr/dot_general | solution.py:27
  141.1 3.6 fusion.64
  144.7 5.1 %fusion.65 = f32[16,128,1024]{2,1,0:T(8,128)} fusion(f32[16,128,1024]{2,1,0:T(8,128)} %get-tuple-element.134, s32[]{:T(128)} %get-tuple-element.133, f32[1024,1024]{1,0:T(8,128)S(1)} %fusion.64, f32[16,128,1024]{2,1,0:T(8,128)} %get-tuple-element.141), kind=kOutput, calls=%fused_computation.5.clone.1 | convolution fusion | flops 1612709888 | bytes 5243904 | tf_op jit(solution)/shard_map/while/body/eval_jaxpr/dot_general | solution.py:27
  149.9 3.6 fusion.64
  153.5 5.1 %fusion.65 = f32[16,128,1024]{2,1,0:T(8,128)} fusion(f32[16,128,1024]{2,1,0:T(8,128)} %get-tuple-element.134, s32[]{:T(128)} %get-tuple-element.133, f32[1024,1024]{1,0:T(8,128)S(1)} %fusion.64, f32[16,128,1024]{2,1,0:T(8,128)} %get-tuple-element.141), kind=kOutput, calls=%fused_computation.5.clone.1 | convolution fusion | flops 1612709888 | bytes 5243904 | tf_op jit(solution)/shard_map/while/body/eval_jaxpr/dot_general | solution.py:27
  158.6 3.6 fusion.64
  162.2 5.1 %fusion.65 = f32[16,128,1024]{2,1,0:T(8,128)} fusion(f32[16,128,1024]{2,1,0:T(8,128)} %get-tuple-element.134, s32[]{:T(128)} %get-tuple-element.133, f32[1024,1024]{1,0:T(8,128)S(1)} %fusion.64, f32[16,128,1024]{2,1,0:T(8,128)} %get-tuple-element.141), kind=kOutput, calls=%fused_computation.5.clone.1 | convolution fusion | flops 1612709888 | bytes 5243904 | tf_op jit(solution)/shard_map/while/body/eval_jaxpr/dot_general | solution.py:27
  167.4 3.6 fusion.64
  171.0 5.2 %fusion.65 = f32[16,128,1024]{2,1,0:T(8,128)} fusion(f32[16,128,1024]{2,1,0:T(8,128)} %get-tuple-element.134, s32[]{:T(128)} %get-tuple-element.133, f32[1024,1024]{1,0:T(8,128)S(1)} %fusion.64, f32[16,128,1024]{2,1,0:T(8,128)} %get-tuple-element.141), kind=kOutput, calls=%fused_computation.5.clone.1 | convolution fusion | flops 1612709888 | bytes 5243904 | tf_op jit(solution)/shard_map/while/body/eval_jaxpr/dot_general | solution.py:27
  176.2 3.6 fusion.64
  179.8 5.1 %fusion.65 = f32[16,128,1024]{2,1,0:T(8,128)} fusion(f32[16,128,1024]{2,1,0:T(8,128)} %get-tuple-element.134, s32[]{:T(128)} %get-tuple-element.133, f32[1024,1024]{1,0:T(8,128)S(1)} %fusion.64, f32[16,128,1024]{2,1,0:T(8,128)} %get-tuple-element.141), kind=kOutput, calls=%fused_computation.5.clone.1 | convolution fusion | flops 1612709888 | bytes 5243904 | tf_op jit(solution)/shard_map/while/body/eval_jaxpr/dot_general | solution.py:27
  184.9 3.6 fusion.64
  188.5 5.1 %fusion.65 = f32[16,128,1024]{2,1,0:T(8,128)} fusion(f32[16,128,1024]{2,1,0:T(8,128)} %get-tuple-element.134, s32[]{:T(128)} %get-tuple-element.133, f32[1024,1024]{1,0:T(8,128)S(1)} %fusion.64, f32[16,128,1024]{2,1,0:T(8,128)} %get-tuple-element.141), kind=kOutput, calls=%fused_computation.5.clone.1 | convolution fusion | flops 1612709888 | bytes 5243904 | tf_op jit(solution)/shard_map/while/body/eval_jaxpr/dot_general | solution.py:27
  193.7 3.6 fusion.64
  197.3 5.1 %fusion.65 = f32[16,128,1024]{2,1,0:T(8,128)} fusion(f32[16,128,1024]{2,1,0:T(8,128)} %get-tuple-element.134, s32[]{:T(128)} %get-tuple-element.133, f32[1024,1024]{1,0:T(8,128)S(1)} %fusion.64, f32[16,128,1024]{2,1,0:T(8,128)} %get-tuple-element.141), kind=kOutput, calls=%fused_computation.5.clone.1 | convolution fusion | flops 1612709888 | bytes 5243904 | tf_op jit(solution)/shard_map/while/body/eval_jaxpr/dot_general | solution.py:27
  202.4 3.6 fusion.64
  206.1 5.1 %fusion.65 = f32[16,128,1024]{2,1,0:T(8,128)} fusion(f32[16,128,1024]{2,1,0:T(8,128)} %get-tuple-element.134, s32[]{:T(128)} %get-tuple-element.133, f32[1024,1024]{1,0:T(8,128)S(1)} %fusion.64, f32[16,128,1024]{2,1,0:T(8,128)} %get-tuple-element.141), kind=kOutput, calls=%fused_computation.5.clone.1 | convolution fusion | flops 1612709888 | bytes 5243904 | tf_op jit(solution)/shard_map/while/body/eval_jaxpr/dot_general | solution.py:27
  211.2 3.6 fusion.64
  214.8 5.1 %fusion.65 = f32[16,128,1024]{2,1,0:T(8,128)} fusion(f32[16,128,1024]{2,1,0:T(8,128)} %get-tuple-element.134, s32[]{:T(128)} %get-tuple-element.133, f32[1024,1024]{1,0:T(8,128)S(1)} %fusion.64, f32[16,128,1024]{2,1,0:T(8,128)} %get-tuple-element.141), kind=kOutput, calls=%fused_computation.5.clone.1 | convolution fusion | flops 1612709888 | bytes 5243904 | tf_op jit(solution)/shard_map/while/body/eval_jaxpr/dot_general | solution.py:27
  220.0 3.6 fusion.64
  223.6 5.1 %fusion.65 = f32[16,128,1024]{2,1,0:T(8,128)} fusion(f32[16,128,1024]{2,1,0:T(8,128)} %get-tuple-element.134, s32[]{:T(128)} %get-tuple-element.133, f32[1024,1024]{1,0:T(8,128)S(1)} %fusion.64, f32[16,128,1024]{2,1,0:T(8,128)} %get-tuple-element.141), kind=kOutput, calls=%fused_computation.5.clone.1 | convolution fusion | flops 1612709888 | bytes 5243904 | tf_op jit(solution)/shard_map/while/body/eval_jaxpr/dot_general | solution.py:27
  228.7 3.6 fusion.64
  232.3 5.1 %fusion.65 = f32[16,128,1024]{2,1,0:T(8,128)} fusion(f32[16,128,1024]{2,1,0:T(8,128)} %get-tuple-element.134, s32[]{:T(128)} %get-tuple-element.133, f32[1024,1024]{1,0:T(8,128)S(1)} %fusion.64, f32[16,128,1024]{2,1,0:T(8,128)} %get-tuple-element.141), kind=kOutput, calls=%fused_computation.5.clone.1 | convolution fusion | flops 1612709888 | bytes 5243904 | tf_op jit(solution)/shard_map/while/body/eval_jaxpr/dot_general | solution.py:27
  237.5 3.6 fusion.64
  241.1 5.1 %fusion.65 = f32[16,128,1024]{2,1,0:T(8,128)} fusion(f32[16,128,1024]{2,1,0:T(8,128)} %get-tuple-element.134, s32[]{:T(128)} %get-tuple-element.133, f32[1024,1024]{1,0:T(8,128)S(1)} %fusion.64, f32[16,128,1024]{2,1,0:T(8,128)} %get-tuple-element.141), kind=kOutput, calls=%fused_computation.5.clone.1 | convolution fusion | flops 1612709888 | bytes 5243904 | tf_op jit(solution)/shard_map/while/body/eval_jaxpr/dot_general | solution.py:27
  246.2 3.6 fusion.64
  249.8 5.2 %fusion.65 = f32[16,128,1024]{2,1,0:T(8,128)} fusion(f32[16,128,1024]{2,1,0:T(8,128)} %get-tuple-element.134, s32[]{:T(128)} %get-tuple-element.133, f32[1024,1024]{1,0:T(8,128)S(1)} %fusion.64, f32[16,128,1024]{2,1,0:T(8,128)} %get-tuple-element.141), kind=kOutput, calls=%fused_computation.5.clone.1 | convolution fusion | flops 1612709888 | bytes 5243904 | tf_op jit(solution)/shard_map/while/body/eval_jaxpr/dot_general | solution.py:27
  255.0 9.3 %copy.21 = f32[1,2048,1024]{2,1,0:T(8,128)} copy(f32[1,2048,1024]{1,2,0:T(8,128)} %get-tuple-element.84) | data formatting | bytes 16777216 | tf_op jit(solution)/shard_map/slice | solution.py:45
  264.3 3.5 fusion.27
  267.8 13.1 %multiply_convert_fusion = bf16[16,128,1024]{2,1,0:T(8,128)(2,1)S(1)} fusion(f32[16,128,1024]{2,1,0:T(8,128)} %bitcast.56, f32[16,128,1024]{2,1,0:T(8,128)} %get-tuple-element.146, f32[16,128,1024]{2,1,0:T(8,128)} %get-tuple-element.70, f32[16,128]{1,0:T(8,128)S(1)} %bitcast.63, f32[16,16,128]{2,1,0:T(8,128)S(1)} %bitcast.61, ...), kind=kOutput, calls=%fused_computation.32 | convolution fusion | flops 413663232 | bytes 29505536 | tf_op jit(solution)/shard_map/htn,hnc->hct/dot_general | solution.py:60
  283.3 95.0 %all_to_all.36 = bf16[16,128,1024]{2,0,1:T(8,128)(2,1)S(1)} all-to-all(bf16[16,128,1024]{2,0,1:T(8,128)(2,1)S(1)} %copy.23), channel_id=1, replica_groups=mesh['ctx'=8,'tp'=4] {'tp'}, dimensions={1} | all-to-all | bytes 8388608 | tf_op jit(solution)/shard_map/all_to_all | solution.py:64
  380.7 52.4 %all_to_all.37 = bf16[64,32,1024]{2,1,0:T(8,128)(2,1)S(1)} all-to-all(bf16[64,32,1024]{2,1,0:T(8,128)(2,1)S(1)} %bitcast.58), channel_id=1, replica_groups=mesh['ctx'=8,'tp'=4] {'ctx'}, dimensions={0} | all-to-all | bytes 8388608 | tf_op jit(solution)/shard_map/all_to_all | solution.py:63
  433.0 2.5 copy.34
  (74 shorter events, 6.7 us)
Async XLA Ops:
  6.5 257.7 %all-gather.3.cloned.1.call-start = ((), (), s32[]{:S(2)}) async-start(), calls=%async_computation.2 | async-start | bytes 1179648 | tf_op jit(solution)/shard_map/all_gather | solution.py:52
  26.0 4.6 %copy-start = (f32[3,3,2048]{2,1,0:T(4,128)S(1)}, f32[3,3,2048]{2,1,0:T(4,128)}, u32[]{:S(2)}) copy-start(f32[3,3,2048]{2,1,0:T(4,128)} %param.12) | copy-start | bytes 221188
  26.0 4.7 %copy-start.1 = (f32[16,16]{1,0:T(8,128)S(1)}, f32[16,16]{1,0:T(8,128)}, u32[]{:S(2)}) copy-start(f32[16,16]{1,0:T(8,128)} %param.14) | copy-start | bytes 3076
  26.9 4.6 %collective-permute-start = (bf16[3,2048,2]{1,2,0:T(2,128)(2,1)S(1)}, bf16[3,2048,2]{1,2,0:T(2,128)(2,1)S(1)}, u32[]{:S(2)}, u32[]{:S(2)}) collective-permute-start(bf16[3,2048,2]{1,2,0:T(2,128)(2,1)S(1)} %pad_maximum_fusion), channel_id=1, source_target_pairs={{0,4},{4,8},{8,12},{12,16},{16,20},{20,24},{24,28},{1,5},{5,9},{9,... | collective-permute-start | bytes 73736 | tf_op jit(solution)/shard_map/ppermute | solution.py:10
  104.5 10.1 %copy-start.2 = (f32[16,16]{1,0:T(8,128)S(1)}, f32[16,16]{1,0:T(8,128)}, u32[]{:S(2)}) copy-start(f32[16,16]{1,0:T(8,128)} %param.15) | copy-start | bytes 3076
  255.0 12.8 %copy-start.3 = (f32[2048]{0:T(1024)S(1)}, f32[2048]{0:T(1024)}, u32[]{:S(2)}) copy-start(f32[2048]{0:T(1024)} %param.13) | copy-start | bytes 24580
Sparse Core Ops, SparseCore 0:
  114.7 25.6 all-gather.2
where the time goes:
time: 448 us; the launch traced here: 442 us
  matrix products  166 us (37%)
  blocking collectives  147 us (33%)
  other arithmetic  64.9 us (14%)
  local copies, waits for them, and re-layouts  45.5 us (10%)
  between operations  13.5 us (3%)
    all_to_all x1, blocking collectives, per_device(): lax.all_to_all(gated, 'tp', split_axis=1, concat_axis=0, tiled=True)  95 us
    dot_general x16, matrix products, near_head(): lax.dot_general(products, toeplitz, (((1,), (1,)), ((), ())), precision=l...  82 us
    dot_general x16, matrix products, near_head(): lax.dot_general(falling, rising, (((0,), (0,)), ((), ())), precision=lax....  57.6 us
    all_to_all x1, blocking collectives, per_device(): lax.all_to_all(lax.all_to_all(gated, 'tp', split_axis=1, concat_axis=0, t...  52.4 us
    add x1, other arithmetic, per_device(): short_filter[:, 0, :, None] * extended[:, :, 2:]  33.9 us
    unnamed x13, local copies, waits for them, and re-layouts  19.6 us
    mul x1, other arithmetic, per_device(): products = (shorted[1] * shorted[2]).reshape(heads_here, head_width, width)  14.9 us
    convert_element_type x1, other arithmetic, per_device(): extended = jnp.concatenate([before, stacked], axis=2).astype(jnp.float32)  14.9 us
  transfers between devices with their start and end apart: 2, of which 1 were waited for; matrix products, arithmetic and copies ran while one was open for 34% of the time, Pallas kernels for 0%

commit v1 on v0

v1 whole, which is shorter than its diff:
```python
import functools

import jax
import jax.numpy as jnp
from jax import lax
from jax.experimental import pallas as pl
from jax.experimental.pallas import tpu as pltpu
from jax.sharding import PartitionSpec as P

LANES = 128
MESH = pl.DeviceIdType.MESH
F32 = jnp.float32
BF16 = jnp.bfloat16


def split2(x):
    high = x.astype(BF16).astype(F32)
    return high, x - high


def kernel(
    size, q_hbm, k_hbm, v_hbm, cols, rate_row, rate_col, weight_col, out,
    qbuf, kbuf, vbuf, halo, phi, plo, acc, sbuf, rbuf, chunk_states, own_states, got_states,
    in_sem, halo_send, halo_recv, st_send, st_recv, a_send, a_recv, b_send, b_recv,
):
    n_ctx, n_tp, heads, hd, width, modes, chunk, group = size
    c = lax.axis_index("ctx")
    z = lax.axis_index("tp")
    ng = heads // group
    rows_g = group * hd
    ratio = n_ctx // n_tp
    heads_out = heads // ratio
    ngo = heads_out // group
    part = hd // n_tp
    nch = width // chunk
    hbms = (k_hbm, v_hbm, q_hbm)
    bufs = (kbuf, vbuf, qbuf)

    def load(f, g):
        rows = pl.ds(pl.multiple_of(g * rows_g, rows_g), rows_g)
        return pltpu.make_async_copy(hbms[f].at[rows], bufs[f].at[rows], in_sem.at[f, g])

    def send_halo(f, g):
        rows = pl.ds(pl.multiple_of(g * rows_g, rows_g), rows_g)
        return pltpu.make_async_remote_copy(
            src_ref=hbms[f].at[rows, pl.ds(width - LANES, LANES)],
            dst_ref=halo.at[f, rows],
            send_sem=halo_send.at[f, g],
            recv_sem=halo_recv.at[f, g],
            device_id={"ctx": lax.rem(c + 1, n_ctx)},
            device_id_type=MESH,
        )

    def send_state(g, to, slot):
        return pltpu.make_async_remote_copy(
            src_ref=own_states.at[pl.ds(g * group, group)],
            dst_ref=got_states.at[slot, pl.ds(g * group, group)],
            send_sem=st_send.at[g, to],
            recv_sem=st_recv.at[g, slot],
            device_id={"ctx": to},
            device_id_type=MESH,
        )

    def send_part(g, to, slot):
        return pltpu.make_async_remote_copy(
            src_ref=sbuf.at[to, pl.ds(g * group, group)],
            dst_ref=rbuf.at[slot, pl.ds(g * group, group)],
            send_sem=a_send.at[to, g],
            recv_sem=a_recv.at[slot, g],
            device_id={"tp": to},
            device_id_type=MESH,
        )

    def place(lg, source):
        return out.at[
            pl.ds(lg * group, group), :, pl.ds(pl.multiple_of(source * width, width), width)
        ]

    def forward_remote(buf, layer, g, source):
        return pltpu.make_async_remote_copy(
            src_ref=buf.at[layer, pl.ds(g * group, group)],
            dst_ref=place(lax.rem(g, ngo), source),
            send_sem=b_send.at[layer, g],
            recv_sem=b_recv.at[source, lax.rem(g, ngo)],
            device_id={"ctx": ratio * layer + g // ngo},
            device_id_type=MESH,
        )

    def forward_local(buf, layer, g):
        return pltpu.make_async_copy(
            buf.at[layer, pl.ds(g * group, group)],
            place(lax.rem(g, ngo), c),
            b_recv.at[c, lax.rem(g, ngo)],
        )

    def forward(buf, layer, g):
        target = ratio * layer + g // ngo

        @pl.when(target != c)
        def _():
            forward_remote(buf, layer, g, c).start()

        @pl.when(target == c)
        def _():
            forward_local(buf, layer, g).start()

    barrier = pltpu.get_barrier_semaphore()

    @pl.loop(1, n_ctx)
    def _(d):
        pl.semaphore_signal(
            barrier, inc=1, device_id={"ctx": lax.rem(c + d, n_ctx)}, device_id_type=MESH
        )

    @pl.loop(1, n_tp)
    def _(d):
        pl.semaphore_signal(
            barrier, inc=1, device_id={"tp": lax.rem(z + d, n_tp)}, device_id_type=MESH
        )

    @pl.loop(0, ng)
    def _(g):
        for f in range(3):
            load(f, g).start()

    @pl.when(c == 0)
    def _():
        halo[...] = jnp.zeros_like(halo)

    pl.semaphore_wait(barrier, n_ctx + n_tp - 2)

    @pl.when(c < n_ctx - 1)
    def _():
        @pl.loop(0, ng)
        def _(g):
            for f in range(3):
                send_halo(f, g).start()

    def ready(f, g):
        load(f, g).wait()

        @pl.when(c > 0)
        def _():
            send_halo(f, g).wait_recv()

    def short(f, coef, first, rows, count):
        x = bufs[f][pl.ds(rows, count), :].astype(F32)
        before = halo[f, pl.ds(rows, count), :].astype(F32)
        whole = jnp.concatenate([before, x], axis=1)
        one = pltpu.roll(whole, 1, 1)[:, LANES:]
        two = pltpu.roll(whole, 2, 1)[:, LANES:]
        return coef[:, first : first + 1] * x + (
            coef[:, first + 1 : first + 2] * one + coef[:, first + 2 : first + 3] * two
        )

    def coefficients(h):
        return cols[:, pl.ds(pl.multiple_of(h * hd, hd), hd)].T

    lane = lax.broadcasted_iota(jnp.int32, (1, chunk), 1).astype(F32)
    spot = lax.broadcasted_iota(jnp.int32, (chunk, 1), 0).astype(F32)
    middle = (chunk - 1.0) * 0.5
    nt = (((1,), (1,)), ((), ()))

    def head_states(h):
        coef = coefficients(h)
        base = pl.multiple_of(h * hd, hd)
        for r in range(0, hd, part):
            some = coef[r : r + part]
            rows = pl.multiple_of(base + r, part)
            p = short(0, some, 3, rows, part) * short(1, some, 6, rows, part)
            high = p.astype(BF16)
            phi[pl.ds(rows, part), :] = high
            plo[pl.ds(rows, part), :] = (p - high.astype(F32)).astype(BF16)
        rate = rate_col[h]
        high, low = split2(jnp.exp(-rate * (chunk - 1.0 - lane)))
        both = jnp.concatenate([high, low], axis=0).astype(BF16)
        p_high = jnp.concatenate(
            [phi[pl.ds(base, hd), j * chunk : (j + 1) * chunk] for j in range(nch)], axis=0
        )
        p_low = jnp.concatenate(
            [plo[pl.ds(base, hd), j * chunk : (j + 1) * chunk] for j in range(nch)], axis=0
        )
        first = lax.dot_general(both, p_high, nt, preferred_element_type=F32)
        second = lax.dot_general(high.astype(BF16), p_low, nt, preferred_element_type=F32)
        total = first[:modes] + (first[modes:] + second)
        chunk_states[h] = total
        step = jnp.exp(-rate * float(chunk))
        state = total[:, :hd]
        for j in range(1, nch):
            state = step * state + total[:, j * hd : (j + 1) * hd]
        own_states[h] = state

    def group_states(g):
        ready(0, g)
        ready(1, g)

        @pl.loop(0, group)
        def _(i):
            head_states(g * group + i)

        @pl.loop(c + 1, n_ctx)
        def _(to):
            send_state(g, to, c).start()

    def head_gated(h):
        coef = coefficients(h)
        base = pl.multiple_of(h * hd, hd)
        rate, weight = rate_col[h], weight_col[h]
        rising = jnp.exp(rate_row[h] * (spot - middle))
        falling = weight * jnp.exp(-rate * (lane - middle))
        full = lax.dot_general(
            rising, falling, (((1,), (0,)), ((), ())),
            precision=lax.Precision.HIGHEST, preferred_element_type=F32,
        )
        causal = lax.broadcasted_iota(jnp.int32, (chunk, chunk), 1) >= lax.broadcasted_iota(
            jnp.int32, (chunk, chunk), 0
        )
        t_high, t_low = split2(jnp.where(causal, full, 0.0))
        t_high, t_low = t_high.astype(BF16), t_low.astype(BF16)
        whole = jnp.exp(-rate * float(width))
        state = lax.fori_loop(
            0, c, lambda k, s: whole * s + got_states[k, h], jnp.zeros((modes, hd), F32)
        )
        step = jnp.exp(-rate * float(chunk))
        mine = chunk_states[h]
        states = [state]
        for j in range(nch - 1):
            states.append(step * states[-1] + mine[:, j * hd : (j + 1) * hd])
        e_high, e_low = split2(jnp.concatenate(states, axis=1))
        e_all = jnp.concatenate([e_high, e_low, e_high], axis=0).T.astype(BF16)
        f_high, f_low = split2(weight * jnp.exp(-rate * (lane + 1.0)))
        f_all = jnp.concatenate([f_high, f_high, f_low], axis=0).astype(BF16)
        p_high = jnp.concatenate(
            [phi[pl.ds(base, hd), j * chunk : (j + 1) * chunk] for j in range(nch)], axis=0
        )
        p_low = jnp.concatenate(
            [plo[pl.ds(base, hd), j * chunk : (j + 1) * chunk] for j in range(nch)], axis=0
        )
        acc[...] = (
            jnp.dot(p_high, t_high, preferred_element_type=F32)
            + jnp.dot(p_low, t_high, preferred_element_type=F32)
            + jnp.dot(p_high, t_low, preferred_element_type=F32)
            + jnp.dot(e_all, f_all, preferred_element_type=F32)
        )
        for r in range(n_tp):
            some = coef[r * part : (r + 1) * part]
            rows = pl.multiple_of(base + r * part, part)
            gate = short(2, some, 0, rows, part)
            p = phi[pl.ds(rows, part), :].astype(F32) + plo[pl.ds(rows, part), :].astype(F32)
            conv = jnp.concatenate(
                [acc[j * hd + r * part : j * hd + (r + 1) * part, :] for j in range(nch)], axis=1
            )
            sbuf[r, h] = (gate * (conv + some[:, 9:10] * p)).astype(BF16)

    def group_gated(g):
        @pl.loop(0, c)
        def _(k):
            send_state(g, c, k).wait_recv()

        ready(2, g)

        @pl.loop(0, group)
        def _(i):
            head_gated(g * group + i)

        @pl.loop(1, n_tp)
        def _(d):
            send_part(g, lax.rem(z + d, n_tp), z).start()

        forward(sbuf, z, g)

    ahead = min(2, ng)
    for g in range(ahead):
        group_states(g)

    @pl.loop(0, ng)
    def _(g):
        group_gated(g)

        @pl.when(g + ahead < ng)
        def _():
            group_states(g + ahead)

    @pl.loop(0, ng)
    def _(g):
        @pl.loop(1, n_tp)
        def _(d):
            layer = lax.rem(z + d, n_tp)
            send_part(g, z, layer).wait_recv()
            forward(rbuf, layer, g)

    @pl.loop(0, ng)
    def _(g):
        @pl.when(c < n_ctx - 1)
        def _():
            for f in range(3):
                send_halo(f, g).wait_send()

        @pl.loop(c + 1, n_ctx)
        def _(to):
            send_state(g, to, c).wait_send()

        @pl.loop(1, n_tp)
        def _(d):
            send_part(g, lax.rem(z + d, n_tp), z).wait_send()

        @pl.loop(0, n_tp)
        def _(layer):
            @pl.when(ratio * layer + g // ngo != c)
            def _():
                forward_remote(rbuf, layer, g, c).wait_send()

    mine = c // ratio
    hout = lax.rem(c, ratio)

    @pl.loop(0, ngo)
    def _(lg):
        g = hout * ngo + lg

        @pl.loop(0, n_ctx)
        def _(source):
            @pl.when(source != c)
            def _():
                forward_remote(rbuf, mine, g, source).wait_recv()

            @pl.when(source == c)
            def _():
                forward_local(rbuf, mine, g).wait()


def per_device(n_ctx, n_tp, query_feat, key_feat, value_feat, short_filter, skip, decay_rate, residue):
    channels, width = query_feat.shape
    heads, modes = decay_rate.shape
    hd = channels // heads
    heads_out = heads * n_tp // n_ctx
    group = 2 if heads_out % 2 == 0 else 1
    chunk = min(256, width)
    ng = heads // group
    ngo = heads_out // group
    part = hd // n_tp
    size = (n_ctx, n_tp, heads, hd, width, modes, chunk, group)
    cols = jnp.concatenate(
        [short_filter.reshape(9, channels), skip[None], jnp.zeros((6, channels), F32)], axis=0
    )
    vmem = pl.BlockSpec(memory_space=pltpu.VMEM)
    hbm = pl.BlockSpec(memory_space=pl.ANY)
    dma = pltpu.SemaphoreType.DMA
    return pl.pallas_call(
        functools.partial(kernel, size),
        out_shape=jax.ShapeDtypeStruct((heads_out, part, width * n_ctx), BF16),
        in_specs=[hbm, hbm, hbm, vmem, vmem, vmem, vmem],
        out_specs=hbm,
        scratch_shapes=[
            pltpu.VMEM((channels, width), BF16),
            pltpu.VMEM((channels, width), BF16),
            pltpu.VMEM((channels, width), BF16),
            pltpu.VMEM((3, channels, LANES), BF16),
            pltpu.VMEM((channels, width), BF16),
            pltpu.VMEM((channels, width), BF16),
            pltpu.VMEM((hd * width // chunk, chunk), F32),
            pltpu.VMEM((n_tp, heads, part, width), BF16),
            pltpu.VMEM((n_tp, heads, part, width), BF16),
            pltpu.VMEM((heads, modes, hd * width // chunk), F32),
            pltpu.VMEM((heads, modes, hd), F32),
            pltpu.VMEM((n_ctx, heads, modes, hd), F32),
            dma((3, ng)),
            dma((3, ng)),
            dma((3, ng)),
            dma((ng, n_ctx)),
            dma((ng, n_ctx)),
            dma((n_tp, ng)),
            dma((n_tp, ng)),
            dma((n_tp, ng)),
            dma((n_ctx, ngo)),
        ],
        compiler_params=pltpu.CompilerParams(
            collective_id=0, has_side_effects=True, vmem_limit_bytes=50 * 1024 * 1024
        ),
        cost_estimate=pl.CostEstimate(
            flops=2 * channels * width * 1024, bytes_accessed=8 * channels * width, transcendentals=0
        ),
    )(
        query_feat, key_feat, value_feat, cols,
        decay_rate[:, None, :], decay_rate[:, :, None], residue[:, :, None],
    )


def solution(mesh):
    return jax.shard_map(
        functools.partial(per_device, mesh.shape["ctx"], mesh.shape["tp"]),
        mesh=mesh,
        in_specs=(
            P("tp", "ctx"),
            P("tp", "ctx"),
            P("tp", "ctx"),
            P(None, None, "tp"),
            P("tp"),
            P("tp", None),
            P("tp", None),
        ),
        out_specs=P("ctx", "tp", None),
        check_vma=False,
    )
```

time: 448 us -> 144 us (0.32)
  the two profiles are of different devices: /device:TPU:11 before, /device:TPU:29 now
where the time goes in v1:
time: 144 us; the launch traced here: 143 us
  Pallas kernels  134 us (93%)
  local copies, waits for them, and re-layouts  8.07 us (6%)
    pallas_call x1, Pallas kernels, per_device(): pl.pallas_call(functools.partial(kernel, size), out_shape=jax.ShapeDtypeS...  134 us
    unnamed x3, local copies, waits for them, and re-layouts  5.34 us

profile of v1, /device:TPU:29, one launch (start us, length us, event | category | flops | bytes accessed | tf_op | source)
XLA Modules:
  0.0 143.3 jit_solution(2286227711433833717)
XLA Ops:
  0.0 0.1 pad.2.clone
  0.1 0.9 reshape.3
  1.0 0.8 maximum_maximum_fusion.cols
  1.8 0.9 copy.9.weight_col
  2.7 0.9 copy.8.rate_col
  3.5 0.0 copy-start
  3.5 0.7 copy-done
  4.2 134.5 %shard_map.73 = bf16[8,32,8192]{2,1,0:T(8,128)(2,1)} custom-call(bf16[2048,1024]{1,0:T(8,128)(2,1)} %q_hbm.1, bf16[2048,1024]{1,0:T(8,128)(2,1)} %k_hbm.1, bf16[2048,1024]{1,0:T(8,128)(2,1)} %v_hbm.1, f32[16,2048]{1,0:T(8,128)S(1)} %maximum_maximum_fusion.cols, f32[16,1,16]{2,1,0:T(1,128)S(1)} %bitcast.5, f32[16,16,1]{2,1,0:T(8,128)S(1)} %copy.8.rate_col, ...), custom_call_target="tpu_custom_call" | custom-call | flops 4294967296 | bytes 16777216 | tf_op jit(solution)/shard_map/pallas_call | solution.py:348
  138.7 4.6 %copy.11 = bf16[8,32,8192]{2,1,0:T(8,128)(2,1)} copy(bf16[8,32,8192]{2,1,0:T(8,128)(2,1)} %shard_map.73) | data formatting | bytes 8388608
  (1 shorter events, 0.0 us)
Async XLA Ops:
  3.5 0.7 copy-start

commit v2 on v1

--- a/solution.py
+++ b/solution.py
@@ -19,9 +19,9 @@
 
 
 def kernel(
-    size, q_hbm, k_hbm, v_hbm, cols, rate_row, rate_col, weight_col, out,
-    qbuf, kbuf, vbuf, halo, phi, plo, acc, sbuf, rbuf, chunk_states, own_states, got_states,
-    in_sem, halo_send, halo_recv, st_send, st_recv, a_send, a_recv, b_send, b_recv,
+    size, q_hbm, k_hbm, v_hbm, filters, skip, decay, residue, out,
+    qbuf, kbuf, vbuf, cols, edge, last, halo, phi, plo, acc, sbuf, rbuf, chunk_states, own_states, got_states,
+    in_sem, edge_sem, halo_send, halo_recv, st_send, st_recv, a_send, a_recv, b_send, b_recv,
 ):
     n_ctx, n_tp, heads, hd, width, modes, chunk, group = size
     c = lax.axis_index("ctx")
@@ -40,13 +40,17 @@
         rows = pl.ds(pl.multiple_of(g * rows_g, rows_g), rows_g)
         return pltpu.make_async_copy(hbms[f].at[rows], bufs[f].at[rows], in_sem.at[f, g])
 
-    def send_halo(f, g):
-        rows = pl.ds(pl.multiple_of(g * rows_g, rows_g), rows_g)
+    def load_edge(f):
+        return pltpu.make_async_copy(
+            hbms[f].at[:, pl.ds(width - LANES, LANES)], edge.at[f], edge_sem.at[f]
+        )
+
+    def send_halo():
         return pltpu.make_async_remote_copy(
-            src_ref=hbms[f].at[rows, pl.ds(width - LANES, LANES)],
-            dst_ref=halo.at[f, rows],
-            send_sem=halo_send.at[f, g],
-            recv_sem=halo_recv.at[f, g],
+            src_ref=last,
+            dst_ref=halo,
+            send_sem=halo_send,
+            recv_sem=halo_recv,
             device_id={"ctx": lax.rem(c + 1, n_ctx)},
             device_id_type=MESH,
         )
@@ -118,34 +122,55 @@
             barrier, inc=1, device_id={"tp": lax.rem(z + d, n_tp)}, device_id_type=MESH
         )
 
+    for f in range(3):
+        load_edge(f).start()
+
     @pl.loop(0, ng)
     def _(g):
         for f in range(3):
             load(f, g).start()
 
+    cols[...] = jnp.zeros_like(cols)
+    for f in range(3):
+        cols[3 * f : 3 * f + 3, :] = filters[f]
+    cols[9:10, :] = skip[...]
+
     @pl.when(c == 0)
     def _():
         halo[...] = jnp.zeros_like(halo)
 
+    row = lax.broadcasted_iota(jnp.int32, (8, LANES), 0)
+    token = lax.broadcasted_iota(jnp.int32, (8, LANES), 1)
+    for f in range(3):
+        load_edge(f).wait()
+
+    @pl.loop(0, heads)
+    def _(h):
+        at = pl.ds(pl.multiple_of(h * hd, hd), hd)
+        picked = jnp.zeros((8, hd), F32)
+        for f in range(3):
+            pick = jnp.where((row >> 1 == f) & (token == LANES - 2 + (row & 1)), 1.0, 0.0)
+            picked = picked + lax.dot_general(
+                pick.astype(BF16), edge[f, at, :], (((1,), (1,)), ((), ())),
+                preferred_element_type=F32,
+            )
+        last[:, at] = picked
+
     pl.semaphore_wait(barrier, n_ctx + n_tp - 2)
 
     @pl.when(c < n_ctx - 1)
     def _():
-        @pl.loop(0, ng)
-        def _(g):
-            for f in range(3):
-                send_halo(f, g).start()
-
-    def ready(f, g):
-        load(f, g).wait()
-
-        @pl.when(c > 0)
-        def _():
-            send_halo(f, g).wait_recv()
+        send_halo().start()
+
+    @pl.when(c > 0)
+    def _():
+        send_halo().wait_recv()
+
+    final = lax.broadcasted_iota(jnp.int32, (part, LANES), 1) == LANES - 1
 
     def short(f, coef, first, rows, count):
         x = bufs[f][pl.ds(rows, count), :].astype(F32)
-        before = halo[f, pl.ds(rows, count), :].astype(F32)
+        before = jnp.where(final, coef[:, 17 + 2 * f : 18 + 2 * f], coef[:, 16 + 2 * f : 17 + 2 * f])
         whole = jnp.concatenate([before, x], axis=1)
         one = pltpu.roll(whole, 1, 1)[:, LANES:]
         two = pltpu.roll(whole, 2, 1)[:, LANES:]
@@ -154,7 +179,15 @@
         )
 
     def coefficients(h):
-        return cols[:, pl.ds(pl.multiple_of(h * hd, hd), hd)].T
+        at = pl.ds(pl.multiple_of(h * hd, hd), hd)
+        return jnp.concatenate([cols[:, at], halo[:, at]], axis=0).T
+
+    diagonal = lax.broadcasted_iota(jnp.int32, (modes, modes), 0) == lax.broadcasted_iota(
+        jnp.int32, (modes, modes), 1
+    )
+
+    def column(ref, h):
+        return jnp.sum(jnp.where(diagonal, ref[pl.ds(h, 1), :], 0.0), axis=1, keepdims=True)
 
     lane = lax.broadcasted_iota(jnp.int32, (1, chunk), 1).astype(F32)
     spot = lax.broadcasted_iota(jnp.int32, (chunk, 1), 0).astype(F32)
@@ -171,7 +204,7 @@
             high = p.astype(BF16)
             phi[pl.ds(rows, part), :] = high
             plo[pl.ds(rows, part), :] = (p - high.astype(F32)).astype(BF16)
-        rate = rate_col[h]
+        rate = column(decay, h)
         high, low = split2(jnp.exp(-rate * (chunk - 1.0 - lane)))
         both = jnp.concatenate([high, low], axis=0).astype(BF16)
         p_high = jnp.concatenate(
@@ -191,8 +224,8 @@
         own_states[h] = state
 
     def group_states(g):
-        ready(0, g)
-        ready(1, g)
+        load(0, g).wait()
+        load(1, g).wait()
 
         @pl.loop(0, group)
         def _(i):
@@ -205,8 +238,8 @@
     def head_gated(h):
         coef = coefficients(h)
         base = pl.multiple_of(h * hd, hd)
-        rate, weight = rate_col[h], weight_col[h]
-        rising = jnp.exp(rate_row[h] * (spot - middle))
+        rate, weight = column(decay, h), column(residue, h)
+        rising = jnp.exp(decay[pl.ds(h, 1), :] * (spot - middle))
         falling = weight * jnp.exp(-rate * (lane - middle))
         full = lax.dot_general(
             rising, falling, (((1,), (0,)), ((), ())),
@@ -257,7 +290,7 @@
         def _(k):
             send_state(g, c, k).wait_recv()
 
-        ready(2, g)
+        load(2, g).wait()
 
         @pl.loop(0, group)
         def _(i):
@@ -267,7 +300,6 @@
         def _(d):
             send_part(g, lax.rem(z + d, n_tp), z).start()
 
-        forward(sbuf, z, g)
 
     ahead = min(2, ng)
     for g in range(ahead):
@@ -283,19 +315,25 @@
 
     @pl.loop(0, ng)
     def _(g):
-        @pl.loop(1, n_tp)
+        @pl.loop(0, n_tp)
         def _(d):
-            layer = lax.rem(z + d, n_tp)
-            send_part(g, z, layer).wait_recv()
-            forward(rbuf, layer, g)
+            layer = lax.rem(c // ratio + d, n_tp)
+
+            @pl.when(layer == z)
+            def _():
+                forward(sbuf, layer, g)
+
+            @pl.when(layer != z)
+            def _():
+                send_part(g, z, layer).wait_recv()
+                forward(rbuf, layer, g)
+
+    @pl.when(c < n_ctx - 1)
+    def _():
+        send_halo().wait_send()
 
     @pl.loop(0, ng)
     def _(g):
-        @pl.when(c < n_ctx - 1)
-        def _():
-            for f in range(3):
-                send_halo(f, g).wait_send()
-
         @pl.loop(c + 1, n_ctx)
         def _(to):
             send_state(g, to, c).wait_send()
@@ -339,9 +377,6 @@
     ngo = heads_out // group
     part = hd // n_tp
     size = (n_ctx, n_tp, heads, hd, width, modes, chunk, group)
-    cols = jnp.concatenate(
-        [short_filter.reshape(9, channels), skip[None], jnp.zeros((6, channels), F32)], axis=0
-    )
     vmem = pl.BlockSpec(memory_space=pltpu.VMEM)
     hbm = pl.BlockSpec(memory_space=pl.ANY)
     dma = pltpu.SemaphoreType.DMA
@@ -354,7 +389,10 @@
             pltpu.VMEM((channels, width), BF16),
             pltpu.VMEM((channels, width), BF16),
             pltpu.VMEM((channels, width), BF16),
+            pltpu.VMEM((16, channels), F32),
             pltpu.VMEM((3, channels, LANES), BF16),
+            pltpu.VMEM((8, channels), F32),
+            pltpu.VMEM((8, channels), F32),
             pltpu.VMEM((channels, width), BF16),
             pltpu.VMEM((channels, width), BF16),
             pltpu.VMEM((hd * width // chunk, chunk), F32),
@@ -364,8 +402,9 @@
             pltpu.VMEM((heads, modes, hd), F32),
             pltpu.VMEM((n_ctx, heads, modes, hd), F32),
             dma((3, ng)),
-            dma((3, ng)),
-            dma((3, ng)),
+            dma((3,)),
+            dma(()),
+            dma(()),
             dma((ng, n_ctx)),
             dma((ng, n_ctx)),
             dma((n_tp, ng)),
@@ -380,8 +419,7 @@
             flops=2 * channels * width * 1024, bytes_accessed=8 * channels * width, transcendentals=0
         ),
     )(
-        query_feat, key_feat, value_feat, cols,
-        decay_rate[:, None, :], decay_rate[:, :, None], residue[:, :, None],
+        query_feat, key_feat, value_feat, short_filter, skip[None], decay_rate, residue
     )
 
 

time: 144 us -> 126 us (0.88)
  the two profiles are of different devices: /device:TPU:29 before, /device:TPU:11 now
where the time goes in v2:
time: 126 us; the launch traced here: 125 us
  Pallas kernels  118 us (94%)
  local copies, waits for them, and re-layouts  7.62 us (6%)
    pallas_call x1, Pallas kernels, per_device(): pl.pallas_call(functools.partial(kernel, size), out_shape=jax.ShapeDtypeS...  118 us
    unnamed x9, local copies, waits for them, and re-layouts  7.62 us

profile of v2, /device:TPU:11, one launch (start us, length us, event | category | flops | bytes accessed | tf_op | source)
XLA Modules:
  0.0 125.5 jit_solution(15832994383962914857)
XLA Ops:
  0.0 0.0 copy-start
  0.0 0.9 copy-done
  0.9 0.0 copy-start.1
  0.9 0.7 copy-done.1
  1.6 0.0 copy-start.2
  1.6 0.7 copy-done.2
  2.3 0.0 copy-start.3
  2.3 0.7 copy-done.3
  3.0 117.8 %shard_map.73 = bf16[8,32,8192]{2,1,0:T(8,128)(2,1)} custom-call(bf16[2048,1024]{1,0:T(8,128)(2,1)} %q_hbm.1, bf16[2048,1024]{1,0:T(8,128)(2,1)} %k_hbm.1, bf16[2048,1024]{1,0:T(8,128)(2,1)} %v_hbm.1, f32[3,3,2048]{2,1,0:T(4,128)S(1)} %copy-done, f32[1,2048]{1,0:T(1,128)S(1)} %bitcast.1, f32[16,16]{1,0:T(8,128)S(1)} %copy-done.2, f32[16,16]{1,0:T(8,128)S(1)} %copy-done.3), custom_call_target="tpu_custom_call" | custom-call | flops 4294967296 | bytes 16777216 | tf_op jit(solution)/shard_map/pallas_call | solution.py:383
  120.8 4.6 %copy.9 = bf16[8,32,8192]{2,1,0:T(8,128)(2,1)} copy(bf16[8,32,8192]{2,1,0:T(8,128)(2,1)} %shard_map.73) | data formatting | bytes 8388608
Async XLA Ops:
  0.0 0.9 copy-start
  0.9 0.7 copy-start.1
  1.6 0.7 copy-start.2
  2.3 0.7 copy-start.3

commit v3 on v2

--- a/solution.py
+++ b/solution.py
@@ -75,6 +75,16 @@
             device_id_type=MESH,
         )
 
+    def send_head(g, i, to, slot):
+        return pltpu.make_async_remote_copy(
+            src_ref=sbuf.at[to, pl.ds(g * group + i, 1)],
+            dst_ref=rbuf.at[slot, pl.ds(g * group + i, 1)],
+            send_sem=a_send.at[to, g],
+            recv_sem=a_recv.at[slot, g],
+            device_id={"tp": to},
+            device_id_type=MESH,
+        )
+
     def place(lg, source):
         return out.at[
             pl.ds(lg * group, group), :, pl.ds(pl.multiple_of(source * width, width), width)
@@ -296,9 +306,9 @@
         def _(i):
             head_gated(g * group + i)
 
-        @pl.loop(1, n_tp)
-        def _(d):
-            send_part(g, lax.rem(z + d, n_tp), z).start()
+            @pl.loop(1, n_tp)
+            def _(d):
+                send_head(g, i, lax.rem(z + d, n_tp), z).start()
 
 
     ahead = min(2, ng)

time: 126 us -> 124 us (0.984)
  Pallas kernels: 118 us -> 116 us
    pallas_call x1, Pallas kernels: 118 us -> 116 us  [per_device(): pl.pallas_call(functools.partial(kernel, size), out_shape=jax.ShapeDtypeS...]
where the time goes in v3:
time: 124 us
  Pallas kernels  116 us (94%)
  local copies, waits for them, and re-layouts  7.62 us (6%)
    pallas_call x1, Pallas kernels, per_device(): pl.pallas_call(functools.partial(kernel, size), out_shape=jax.ShapeDtypeS...  116 us
    unnamed x9, local copies, waits for them, and re-layouts  7.62 us

profile of v3, /device:TPU:11, one launch (start us, length us, event | category | flops | bytes accessed | tf_op | source)
XLA Modules:
  0.0 123.8 jit_solution(18140675436088728861)
XLA Ops:
  0.0 0.0 copy-start
  0.0 0.9 copy-done
  0.9 0.0 copy-start.1
  0.9 0.7 copy-done.1
  1.6 0.0 copy-start.2
  1.6 0.7 copy-done.2
  2.3 0.0 copy-start.3
  2.3 0.7 copy-done.3
  3.0 116.2 %shard_map.73 = bf16[8,32,8192]{2,1,0:T(8,128)(2,1)} custom-call(bf16[2048,1024]{1,0:T(8,128)(2,1)} %q_hbm.1, bf16[2048,1024]{1,0:T(8,128)(2,1)} %k_hbm.1, bf16[2048,1024]{1,0:T(8,128)(2,1)} %v_hbm.1, f32[3,3,2048]{2,1,0:T(4,128)S(1)} %copy-done, f32[1,2048]{1,0:T(1,128)S(1)} %bitcast.1, f32[16,16]{1,0:T(8,128)S(1)} %copy-done.2, f32[16,16]{1,0:T(8,128)S(1)} %copy-done.3), custom_call_target="tpu_custom_call" | custom-call | flops 4294967296 | bytes 16777216 | tf_op jit(solution)/shard_map/pallas_call | solution.py:393
  119.2 4.6 %copy.9 = bf16[8,32,8192]{2,1,0:T(8,128)(2,1)} copy(bf16[8,32,8192]{2,1,0:T(8,128)(2,1)} %shard_map.73) | data formatting | bytes 8388608
Async XLA Ops:
  0.0 0.9 copy-start
  0.9 0.7 copy-start.1
  1.6 0.7 copy-start.2
  2.3 0.7 copy-start.3
